TPU v7x, 32 devices: a whole 2x2x4 slice. The times are simulated.
32 devices in a mesh: lon: 16 (over z, x, core), tp: 2 (over y).
Axes of the slice: x: 2, y: 2, z: 4, core: 2. Of those that a mesh axis runs over, the one named last changes fastest.
Arguments:
- image_tokens: bfloat16 [4096, 3072], P('lon', 'tp'), may hold values from -6 to 6
- style_tokens: bfloat16 [512, 3072], P('lon', 'tp'), may hold values from -6 to 6
- qkv_weight: bfloat16 [3, 3072, 2048], P(None, 'lon', 'tp'), may hold values from -0.109375 to 0.109375
- out_weight: bfloat16 [2048, 3072], P('tp', 'lon'), may hold values from -0.125 to 0.125
- query_gain: float32 [128], replicated, may hold values from 0.6 to 9, as said below
- key_gain: float32 [128], replicated, may hold values from 0.6 to 9, as said below
- attend_flags: int32 [16, 1], P('lon'), may hold values from 0 to 1
Outputs:
- mixed: bfloat16 [4096, 3072], P('lon', 'tp')
Inputs may be any that keep to these rules, and one draw needn't show every extreme that they name: `query_gain`: positive gains. `key_gain`: positive gains.
All inputs are finite; a program needn't handle non-finite values.
Results may differ from a plain program's by a relative error of at most 0.015.
The roundings to bfloat16 on the way count: a program that leaves them out, or rounds other values in their place, can miss the bound.
Values may be sent and summed in bfloat16 or wider, within the bound.
A program may use at most 64 MiB of HBM per device.

v0:
```python
import math

import jax
import jax.numpy as jnp
from jax import lax
from jax.sharding import PartitionSpec as P

HEAD = 128


def with_halo(block, sides, width):
    for axis, dim in sides:
        count = lax.axis_size(axis)
        forward = [(i, i + 1) for i in range(count - 1)]
        forward.append((count - 1, 0))
        backward = [(target, source) for source, target in forward]
        low = lax.ppermute(
            lax.slice_in_dim(block, block.shape[dim] - width, None, axis=dim), axis, forward
        )
        high = lax.ppermute(lax.slice_in_dim(block, 0, width, axis=dim), axis, backward)
        block = jnp.concatenate([low, block, high], axis=dim)
    return block


def head_norm(values, gain):
    return values * lax.rsqrt(jnp.mean(values * values, axis=-1, keepdims=True) + 1e-06) * gain


def local(image_tokens, style_tokens, qkv_weight, out_weight, query_gain, key_gain, attend_flags):
    count = image_tokens.shape[0]
    ref_local = style_tokens.shape[0]
    width_here = qkv_weight.shape[2]
    heads_here = width_here // HEAD
    image_full, style_full = (
        lax.all_gather(image_tokens, "tp", axis=1, tiled=True),
        lax.all_gather(style_tokens, "tp", axis=1, tiled=True),
    )
    panel = lax.all_gather(qkv_weight, "lon", axis=1, tiled=True)
    projected = jnp.einsum("td,jdc->jtc", image_full, panel, preferred_element_type=jnp.float32)
    style_proj = jnp.einsum(
        "td,jdc->jtc", style_full, panel[1:], preferred_element_type=jnp.float32
    )
    query = head_norm(projected[0].reshape(count, heads_here, HEAD), query_gain).astype(
        jnp.bfloat16
    )
    keys = head_norm(projected[1].reshape(count, heads_here, HEAD), key_gain).astype(jnp.bfloat16)
    values = projected[2].astype(jnp.bfloat16)
    own_pair = jnp.stack([keys.reshape(count, width_here), values])
    style_key = head_norm(style_proj[0].reshape(ref_local, heads_here, HEAD), key_gain).astype(
        jnp.bfloat16
    )
    style_pair = jnp.stack(
        [style_key.reshape(ref_local, width_here), style_proj[1].astype(jnp.bfloat16)]
    )
    widened = with_halo(own_pair, (("lon", 1),), count)
    style_all = lax.all_gather(style_pair, "lon", axis=1, tiled=True)
    ref_total = style_all.shape[1]
    key_set = jnp.concatenate([widened[0], style_all[0]], axis=0).reshape(-1, heads_here, HEAD)
    value_set = jnp.concatenate([widened[1], style_all[1]], axis=0).reshape(-1, heads_here, HEAD)
    flags = attend_flags[0]
    allowed = jnp.concatenate([jnp.ones((3 * count,), bool), jnp.full((ref_total,), flags[0] > 0)])
    scores = jnp.einsum(
        "qhe,khe->hqk", query, key_set, preferred_element_type=jnp.float32
    ) / math.sqrt(HEAD)
    scores = jnp.where(allowed[None, None, :], scores, -1e30)
    peak = jnp.max(scores, axis=-1, keepdims=True)
    expo = jnp.exp(scores - peak)
    weights = (expo / jnp.sum(expo, axis=-1, keepdims=True)).astype(jnp.bfloat16)
    attended = jnp.einsum("hqk,khe->qhe", weights, value_set, preferred_element_type=jnp.float32)
    attended = attended.astype(jnp.bfloat16).reshape(count, width_here)
    partial_sums = jnp.dot(
        attended,
        lax.all_gather(out_weight, "lon", axis=1, tiled=True),
        preferred_element_type=jnp.float32,
    )
    return lax.psum_scatter(
        partial_sums.astype(jnp.bfloat16), "tp", scatter_dimension=1, tiled=True
    )


def solution(mesh):
    in_specs = (
        P("lon", "tp"),
        P("lon", "tp"),
        P(None, "lon", "tp"),
        P("tp", "lon"),
        P(),
        P(),
        P("lon", None),
    )
    out_specs = P("lon", "tp")
    return jax.shard_map(local, mesh=mesh, in_specs=in_specs, out_specs=out_specs, check_vma=False)
```

profile of v0, /device:TPU:0, one launch (start us, length us, event | category | flops | bytes accessed | tf_op | source)
XLA Modules:
  0.0 292.7 jit_solution(11363684699807901159)
XLA Ops:
  6.5 0.7 all-gather.5.cloned.1.call-update
  7.3 0.7 all-gather.7.cloned.1.call-update
  8.1 6.7 %all_gather.17 = bf16[32,3072]{1,0:T(8,128)(2,1)S(1)} all-gather(bf16[32,1536]{1,0:T(8,128)(2,1)} %param.8), channel_id=1, replica_groups=mesh['lon'=16,'tp'=2] {'tp'}, dimensions={1}, use_global_device_ids=true | all-gather | bytes 294912 | tf_op jit(solution)/shard_map/all_gather | solution.py:36
  14.8 95.8 %all-gather.5.cloned.1.call-done = bf16[3,3072,1024]{2,1,0:T(8,128)(2,1)} async-done(((bf16[3,192,1024]{2,1,0:T(8,128)(2,1)}), bf16[3,3072,1024]{2,1,0:T(8,128)(2,1)}) %all-gather.5.cloned.1.call-update) | async-done | bytes 18874384 | tf_op jit(solution)/shard_map/all_gather | solution.py:38
  110.6 5.7 %fusion.19 = f32[2,32,1024]{2,1,0:T(8,128)S(1)} fusion(bf16[3,3072,1024]{2,1,0:T(8,128)(2,1)} %all-gather.5.cloned.1.call-done, bf16[32,3072]{1,0:T(8,128)(2,1)S(1)} %all_gather.17), kind=kOutput, calls=%fused_computation.23 | convolution fusion | flops 402653184 | bytes 13041664 | tf_op jit(solution)/shard_map/td,jdc->jtc/dot_general | solution.py:40
  116.3 0.1 reduce_sum.37
  116.5 0.1 mul.98
  116.6 0.7 pad_maximum_fusion.2
  117.4 0.5 all-gather.11.cloned.1.call-update
  117.9 21.4 %all-gather.7.cloned.1.call-done = bf16[256,3072]{1,0:T(8,128)(2,1)} async-done(((bf16[256,1536]{1,0:T(8,128)(2,1)}), bf16[256,3072]{1,0:T(8,128)(2,1)}) %all-gather.7.cloned.1.call-update) | async-done | bytes 1572880 | tf_op jit(solution)/shard_map/all_gather | solution.py:35
  139.4 9.8 %convolution_bitcast_fusion = f32[3,256,1024]{1,2,0:T(8,128)S(1)} fusion(bf16[3,3072,1024]{2,1,0:T(8,128)(2,1)} %all-gather.5.cloned.1.call-done, bf16[256,3072]{1,0:T(8,128)(2,1)} %all-gather.7.cloned.1.call-done), kind=kOutput, calls=%fused_computation.20 | convolution fusion | flops 4831838208 | bytes 23592960 | tf_op jit(solution)/shard_map/td,jdc->jtc/dot_general | solution.py:39
  149.2 1.6 copy-done.2
  150.9 1.8 fusion.38
  152.7 0.1 pad_maximum_fusion.1
  152.8 3.7 %collective-permute-start.1 = (bf16[2,256,1024]{1,2,0:T(8,128)(2,1)S(1)}, bf16[2,256,1024]{1,2,0:T(8,128)(2,1)}, u32[]{:S(2)}, u32[]{:S(2)}) collective-permute-start(bf16[2,256,1024]{1,2,0:T(8,128)(2,1)S(1)} %pad_maximum_fusion.1), channel_id=1, source_target_pairs={{2,0},{4,2},{6,4},{8,6},{10,8},{12,10},{14,12},{16,14},{18,16},{20... | collective-permute-start | bytes 3145736 | tf_op jit(solution)/shard_map/ppermute | solution.py:20
  157.2 1.4 copy.9
  158.6 0.1 multiply_reduce_fusion
  158.7 11.1 %collective-permute-done.1 = bf16[2,256,1024]{1,2,0:T(8,128)(2,1)} collective-permute-done((bf16[2,256,1024]{1,2,0:T(8,128)(2,1)S(1)}, bf16[2,256,1024]{1,2,0:T(8,128)(2,1)}, u32[]{:S(2)}, u32[]{:S(2)}) %collective-permute-start.1) | collective-permute-done | bytes 1048608 | tf_op jit(solution)/shard_map/ppermute | solution.py:20
  169.8 4.5 %collective-permute-done = bf16[2,256,1024]{1,2,0:T(8,128)(2,1)} collective-permute-done((bf16[2,256,1024]{1,2,0:T(8,128)(2,1)S(1)}, bf16[2,256,1024]{1,2,0:T(8,128)(2,1)}, u32[]{:S(2)}, u32[]{:S(2)}) %collective-permute-start) | collective-permute-done | bytes 1048608 | tf_op jit(solution)/shard_map/ppermute | solution.py:17
  174.3 1.6 pad_maximum_fusion
  175.9 1.4 fusion.37
  177.3 0.9 copy.10
  178.2 14.4 %all-gather.9.cloned.1.call-done = bf16[2,512,1024]{2,1,0:T(8,128)(2,1)} async-done(((bf16[2,32,1024]{2,1,0:T(8,128)(2,1)}), bf16[2,512,1024]{2,1,0:T(8,128)(2,1)}) %all-gather.9.cloned.1.call-update) | async-done | bytes 2097168 | tf_op jit(solution)/shard_map/all_gather | solution.py:56
  192.6 1.7 fusion.39
  194.4 0.3 copy.14
  194.6 1.2 copy.11
  195.8 1.3 copy.12
  197.2 7.5 %fusion.40 = (f32[8,256]{1,0:T(8,128)S(1)}, f32[8,256,1280]{2,1,0:T(8,128)}) fusion(pred[1280]{0:T(1024)(128)(4,1)S(1)} %concatenate.26, bf16[512,8,128]{2,0,1:T(8,128)(2,1)} %copy.11, bf16[768,8,128]{2,0,1:T(8,128)(2,1)S(1)} %copy.10, f32[256,8,128]{2,0,1:T(8,128)} %copy.9, f32[128]{0:T(128)S(1)} %copy-done.4, f32[256,8]{0,1:T(8,128)S(1)} %add_rsqrt_fusion.1), kind=kOutput, calls=%fused_computation.50 | convolution fusion | flops 687604992 | bytes 14173952 | tf_op jit(solution)/shard_map/sub | solution.py:67
  204.6 6.3 %fusion.16 = bf16[8,128,256]{2,1,0:T(8,128)(2,1)S(1)} fusion(f32[8,256,1280]{2,1,0:T(8,128)} %get-tuple-element.12, f32[8,256]{1,0:T(8,128)S(1)} %get-tuple-element.11, bf16[512,8,128]{0,2,1:T(8,128)(2,1)} %bitcast.44, bf16[768,8,128]{0,2,1:T(8,128)(2,1)S(1)} %bitcast.43), kind=kOutput, calls=%fused_computation.22 | convolution fusion | flops 681836544 | bytes 13639680 | tf_op jit(solution)/shard_map/hqk,khe->qhe/dot_general | solution.py:69
  210.9 44.5 %all-gather.11.cloned.1.call-done = bf16[1024,3072]{0,1:T(8,128)(2,1)} async-done(((bf16[1024,192]{0,1:T(8,128)(2,1)}), bf16[1024,3072]{0,1:T(8,128)(2,1)}) %all-gather.11.cloned.1.call-update) | async-done | bytes 6291472 | tf_op jit(solution)/shard_map/all_gather | solution.py:73
  255.5 5.8 %convolution_convert_fusion = bf16[256,3072]{1,0:T(8,128)(2,1)} fusion(bf16[256,1024]{0,1:T(8,128)(2,1)S(1)} %bitcast.46, bf16[1024,3072]{0,1:T(8,128)(2,1)} %all-gather.11.cloned.1.call-done), kind=kOutput, calls=%fused_computation.11 | convolution fusion | flops 1611399168 | bytes 8388608 | tf_op jit(solution)/shard_map/dot_general | solution.py:71
  261.3 24.8 %reduce-scatter.2.cloned.1.call-done = bf16[256,1536]{1,0:T(8,128)(2,1)} async-done(((bf16[256,3072]{1,0:T(8,128)(2,1)}), bf16[256,1536]{1,0:T(8,128)(2,1)}) %reduce-scatter.2.cloned.1.call-update) | async-done | bytes 786448 | tf_op jit(solution)/shard_map/reduce_scatter | solution.py:76
  (31 shorter events, 0.6 us)
Async XLA Ops:
  6.5 8.2 %copy-start = (f32[128]{0:T(128)S(1)}, f32[128]{0:T(128)}, u32[]{:S(2)}) copy-start(f32[128]{0:T(128)} %param.12) | copy-start | bytes 1540
  6.5 104.0 %all-gather.5.cloned.1.call-start = ((), (), s32[]{:S(2)}) async-start(), calls=%async_computation.1 | async-start | bytes 20054016 | tf_op jit(solution)/shard_map/all_gather | solution.py:38
  7.3 132.1 %all-gather.7.cloned.1.call-start = ((), (), s32[]{:S(2)}) async-start(), calls=%async_computation.2 | async-start | bytes 2359296 | tf_op jit(solution)/shard_map/all_gather | solution.py:35
  8.0 184.6 %all-gather.9.cloned.1.call-start = ((), (), s32[]{:S(2)}) async-start(), calls=%async_computation.3 | async-start | bytes 2228224 | tf_op jit(solution)/shard_map/all_gather | solution.py:56
  117.3 138.2 %all-gather.11.cloned.1.call-start = ((), (), s32[]{:S(2)}) async-start(), calls=%async_computation.4 | async-start | bytes 6684672 | tf_op jit(solution)/shard_map/all_gather | solution.py:73
  117.9 168.3 %reduce-scatter.2.cloned.1.call-start = ((), (), s32[]{:S(2)}) async-start(), calls=%async_computation.5 | async-start | bytes 2359296 | tf_op jit(solution)/shard_map/reduce_scatter | solution.py:76
  149.1 1.6 copy-start.2
  152.8 16.9 %collective-permute-start.1 = (bf16[2,256,1024]{1,2,0:T(8,128)(2,1)S(1)}, bf16[2,256,1024]{1,2,0:T(8,128)(2,1)}, u32[]{:S(2)}, u32[]{:S(2)}) collective-permute-start(bf16[2,256,1024]{1,2,0:T(8,128)(2,1)S(1)} %pad_maximum_fusion.1), channel_id=1, source_target_pairs={{2,0},{4,2},{6,4},{8,6},{10,8},{12,10},{14,12},{16,14},{18,16},{20... | collective-permute-start | bytes 3145736 | tf_op jit(solution)/shard_map/ppermute | solution.py:20
  156.6 17.7 %collective-permute-start = (bf16[2,256,1024]{1,2,0:T(8,128)(2,1)S(1)}, bf16[2,256,1024]{1,2,0:T(8,128)(2,1)}, u32[]{:S(2)}, u32[]{:S(2)}) collective-permute-start(bf16[2,256,1024]{1,2,0:T(8,128)(2,1)S(1)} %pad_maximum_fusion.1), channel_id=1, source_target_pairs={{0,2},{2,4},{4,6},{6,8},{8,10},{10,12},{12,14},{14,16},{16,18},{18... | collective-permute-start | bytes 3145736 | tf_op jit(solution)/shard_map/ppermute | solution.py:17
  178.2 19.0 %copy-start.4 = (f32[128]{0:T(128)S(1)}, f32[128]{0:T(128)}, u32[]{:S(2)}) copy-start(f32[128]{0:T(128)} %param.11) | copy-start | bytes 1540
  197.2 7.5 %copy-start.3 = (bf16[1,768,1024]{1,2,0:T(8,128)(2,1)S(1)}, bf16[1,768,1024]{1,2,0:T(8,128)(2,1)}, u32[]{:S(2)}) copy-start(bf16[1,768,1024]{1,2,0:T(8,128)(2,1)} %get-tuple-element.5) | copy-start | bytes 4718596
  255.5 30.7 %copy-start.1 = (f32[128]{0:T(128)S(1)}, f32[128]{0:T(128)}, u32[]{:S(2)}) copy-start(f32[128]{0:T(128)} %param.12) | copy-start | bytes 1540
Sparse Core Ops, SparseCore 0:
  8.9 101.6 all-gather.4
  112.1 27.2 all-gather.6
  141.5 51.0 all-gather.8
  194.8 60.6 all-gather.10
  261.5 24.6 reduce-scatter.1
where the time goes:
time: 293 us
  waiting for transfers between devices  219 us (75%)
  matrix products  35.1 us (12%)
  between operations  14 us (5%)
  local copies, waits for them, and re-layouts  9.95 us (3%)
  blocking collectives  6.69 us (2%)
  other arithmetic  4.58 us (2%)
  starting transfers between devices  3.89 us (1%)
    all_gather x1, waiting for transfers between devices, local(): panel = lax.all_gather(qkv_weight, 'lon', axis=1, tiled=True)  95.8 us
    all_gather x1, waiting for transfers between devices, local(): lax.all_gather(out_weight, 'lon', axis=1, tiled=True)  44.5 us
    reduce_scatter x1, waiting for transfers between devices, local(): lax.psum_scatter(partial_sums.astype(jnp.bfloat16), 'tp', scatter_dimensi...  24.8 us
    all_gather x1, waiting for transfers between devices, local(): lax.all_gather(image_tokens, 'tp', axis=1, tiled=True)  21.4 us
    all_gather x1, waiting for transfers between devices, local(): style_all = lax.all_gather(style_pair, 'lon', axis=1, tiled=True)  14.4 us
    ppermute x1, waiting for transfers between devices, with_halo(): lax.ppermute(lax.slice_in_dim(block, 0, width, axis=dim), axis, backward)  11.1 us
    dot_general x1, matrix products, local(): jnp.einsum('td,jdc->jtc', image_full, panel, preferred_element_type=jnp.f...  9.77 us
    sub x1, matrix products, local(): expo = jnp.exp(scores - peak)  7.48 us
  transfers between devices with their start and end apart: 7, of which 7 were waited for; matrix products, arithmetic and copies ran while one was open for 14% of the time, Pallas kernels for 0%

commit v1 on v0

v1 whole, which is shorter than its diff:
```python
import functools
import math

import jax
import jax.numpy as jnp
from jax import lax
from jax.experimental import pallas as pl
from jax.experimental.pallas import tpu as pltpu
from jax.sharding import PartitionSpec as P

HEAD = 128
ITEMS = 5
MESH = pl.DeviceIdType.MESH
NT = (((1,), (1,)), ((), ()))


def normed(part, gain):
    return part * lax.rsqrt(jnp.mean(part * part, axis=-1, keepdims=True) + 1e-06) * gain


def kernel(
    n_lon,
    n_tp,
    image_ref,
    style_ref,
    qkv_ref,
    out_w_ref,
    query_gain_ref,
    key_gain_ref,
    flags_ref,
    mixed_ref,
    tokens,
    styles,
    weights,
    queries,
    keys,
    values,
    probs,
    attended,
    part,
    arrived,
    ring_send,
    ring_recv,
    sib_send,
    sib_recv,
    own_send,
    own_recv,
    tp_send,
    tp_recv,
    halo_send,
    halo_recv,
    fwd_send,
    fwd_recv,
    out_send,
    out_recv,
):
    count, feat = image_ref.shape
    style_rows = style_ref.shape[0]
    block = qkv_ref.shape[1]
    width = qkv_ref.shape[2]
    heads = width // HEAD
    key_count = keys.shape[0]
    outw = mixed_ref.shape[1]
    chips = n_lon // 2
    half_ring = chips // 2
    lon = lax.axis_index("lon")
    tp = lax.axis_index("tp")
    chip = lon // 2
    core = lon % 2
    odd = chip % 2
    place = (1 - odd) * (chip // 2) + odd * (chips - (chip + 1) // 2)

    def lon_at(position, side):
        position = lax.rem(position + 2 * chips, chips)
        upper = position // half_ring
        there = (1 - upper) * (2 * position) + upper * (2 * chips - 1 - 2 * position)
        return there * 2 + side

    right = {"lon": lon_at(place + 1, core)}
    left = {"lon": lon_at(place - 1, core)}
    sibling = {"lon": chip * 2 + 1 - core}
    after = {"lon": lax.rem(lon + 1, n_lon)}
    before = {"lon": lax.rem(lon + n_lon - 1, n_lon)}
    peers = [{"tp": lax.rem(tp + k, n_tp)} for k in range(1, n_tp)]

    low_w = block // 2 // 16 * 16
    low_s = style_rows // 2 // 16 * 16

    def slot(item, owner, half):
        if item == 0:
            total, low = style_rows, low_s
        else:
            total, low = block, low_w
        start, size = {0: (0, low), 1: (low, total - low), 2: (0, total)}[half]
        if item == 0:
            return styles.at[tp, owner % 2, owner // 2, pl.ds(start, size), :]
        return weights.at[item - 1, pl.ds(pl.multiple_of(owner * block, 16) + start, size), :]

    barrier = pltpu.get_barrier_semaphore()
    partners = [right, left, sibling, after, before] + peers
    for partner in partners:
        pl.semaphore_signal(barrier, inc=1, device_id=partner, device_id_type=MESH)

    styles[tp, core, chip] = style_ref[...]
    tokens[tp] = image_ref[...]
    own_rows = pl.ds(pl.multiple_of(lon * block, 16), block)
    for j in range(3):
        weights[j, own_rows, :] = qkv_ref[j]
    weights[3, own_rows, :] = out_w_ref[...]
    pl.semaphore_wait(barrier, len(partners))

    started = []

    def send(src, dst, send_sem, recv_sem, device):
        copy = pltpu.make_async_remote_copy(
            src_ref=src,
            dst_ref=dst,
            send_sem=send_sem,
            recv_sem=recv_sem,
            device_id=device,
            device_id_type=MESH,
        )
        copy.start()
        started.append(copy)

    def await_recv(dst, send_sem, recv_sem, device):
        pltpu.make_async_remote_copy(
            src_ref=dst,
            dst_ref=dst,
            send_sem=send_sem,
            recv_sem=recv_sem,
            device_id=device,
            device_id_type=MESH,
        ).wait_recv()

    per_item = chips - 1
    total = ITEMS * per_item

    def piece(index, direction):
        item, at = divmod(index, per_item)
        hop, second = divmod(at, 2)
        half = second if direction == 0 else 1 - second
        return item, hop, half

    def origin(hop, direction, side):
        return lon_at(place - hop if direction == 0 else place + hop, side)

    def ring_step(index):
        got = index - 2
        if 0 <= got < total:
            for direction in range(2):
                item, hop, half = piece(got, direction)
                ref = slot(item, origin(hop + 1, direction, core), half)
                device = right if direction == 0 else left
                await_recv(ref, ring_send.at[direction, got], ring_recv.at[direction, got], device)
                send(ref, ref, sib_send.at[direction, got], sib_recv.at[direction, got], sibling)
        if index < total:
            for direction in range(2):
                item, hop, half = piece(index, direction)
                ref = slot(item, origin(hop, direction, core), half)
                device = right if direction == 0 else left
                send(
                    ref,
                    ref,
                    ring_send.at[direction, index],
                    ring_recv.at[direction, index],
                    device,
                )

    def await_sibling(item):
        ref = slot(item, chip * 2 + 1 - core, 2)
        await_recv(ref, own_send.at[item], own_recv.at[item], sibling)
        for at in range(per_item):
            index = item * per_item + at
            for direction in range(2):
                _, hop, half = piece(index, direction)
                ref = slot(item, origin(hop + 1, direction, 1 - core), half)
                await_recv(
                    ref, sib_send.at[direction, index], sib_recv.at[direction, index], sibling
                )

    tile = 512 if width % 512 == 0 else width

    def project(source, j, write):
        @pl.loop(0, width // tile)
        def _(at):
            start = pl.multiple_of(at * tile, tile)
            acc = None
            for t in range(n_tp):
                term = jnp.dot(
                    source(t),
                    weights[j, t * feat : (t + 1) * feat, pl.ds(start, tile)],
                    preferred_element_type=jnp.float32,
                )
                acc = term if acc is None else acc + term
            write(start, acc)

    def write_normed(dst, row, gain_ref):
        def write(start, acc):
            gain = gain_ref[...]
            for h in range(tile // HEAD):
                dst[row : row + acc.shape[0], pl.ds(start + h * HEAD, HEAD)] = normed(
                    acc[:, h * HEAD : (h + 1) * HEAD], gain
                ).astype(jnp.bfloat16)

        return write

    def write_plain(dst, row):
        def write(start, acc):
            dst[row : row + acc.shape[0], pl.ds(start, tile)] = acc.astype(jnp.bfloat16)

        return write

    def own_tokens(t):
        return tokens[t]

    def style_tokens_of(t):
        return styles[t].reshape(n_lon * style_rows, feat)

    def send_halo(ref, which):
        own = ref.at[pl.ds(count, count), :]
        for side, device in ((0, after), (1, before)):
            send(
                own,
                ref.at[pl.ds(2 * count * side, count), :],
                halo_send.at[which, side],
                halo_recv.at[which, side],
                device,
            )

    def await_halo(ref, which):
        for side, device in ((0, after), (1, before)):
            await_recv(
                ref.at[pl.ds(2 * count * side, count), :],
                halo_send.at[which, side],
                halo_recv.at[which, side],
                device,
            )

    def at_style():
        for k, device in enumerate(peers):
            ref = styles.at[tp, core]
            send(ref, ref, tp_send.at[1, k], tp_recv.at[1, k], device)

    def at_query():
        await_sibling(1)
        for k, device in enumerate(peers):
            ref = tokens.at[lax.rem(tp + n_tp - 1 - k, n_tp)]
            await_recv(ref, tp_send.at[0, k], tp_recv.at[0, k], device)
        project(own_tokens, 0, write_normed(queries, 0, query_gain_ref))

    def at_style_peers():
        for k, device in enumerate(peers):
            ref = styles.at[lax.rem(tp + n_tp - 1 - k, n_tp), core]
            await_recv(ref, tp_send.at[1, k], tp_recv.at[1, k], device)
            send(ref, ref, fwd_send.at[k], fwd_recv.at[k], sibling)

    def at_key():
        await_sibling(2)
        project(own_tokens, 1, write_normed(keys, count, key_gain_ref))
        send_halo(keys, 0)

    def at_style_key():
        await_sibling(0)
        for k in range(n_tp - 1):
            ref = styles.at[lax.rem(tp + n_tp - 1 - k, n_tp), 1 - core]
            await_recv(ref, fwd_send.at[k], fwd_recv.at[k], sibling)
        project(style_tokens_of, 1, write_normed(keys, 3 * count, key_gain_ref))

    def score(first, last):
        bias = jnp.where(flags_ref[0, 0] > 0, 0.0, -1e30).astype(jnp.float32)
        spot = lax.broadcasted_iota(jnp.int32, (1, key_count), 1)
        row = jnp.where(spot < 3 * count, 0.0, bias)

        @pl.loop(first, last)
        def _(h):
            cols = pl.ds(pl.multiple_of(h * HEAD, HEAD), HEAD)
            s = lax.dot_general(
                queries[:, cols], keys[:, cols], NT, preferred_element_type=jnp.float32
            )
            s = s * (1.0 / math.sqrt(HEAD)) + row
            expo = jnp.exp(s - jnp.max(s, axis=-1, keepdims=True))
            inverse = 1.0 / jnp.sum(expo, axis=-1, keepdims=True)
            probs[h] = (expo * inverse).astype(jnp.bfloat16)

    def at_value():
        await_sibling(3)
        project(own_tokens, 2, write_plain(values, count))
        send_halo(values, 1)

    def at_style_value():
        project(style_tokens_of, 2, write_plain(values, 3 * count))

    def attend():
        await_halo(values, 1)

        @pl.loop(0, heads)
        def _(h):
            cols = pl.ds(pl.multiple_of(h * HEAD, HEAD), HEAD)
            attended[:, cols] = jnp.dot(
                probs[h], values[:, cols], preferred_element_type=jnp.float32
            ).astype(jnp.bfloat16)

    pair = max(heads // 4, 1)

    def score_part(quarter):
        if quarter == 0:
            await_halo(keys, 0)
        if quarter * pair < heads:
            score(quarter * pair, quarter * pair + pair)

    hooks = {
        per_item + 2: [at_style],
        2 * per_item + 2: [at_query],
        2 * per_item + 4: [at_style_peers],
        3 * per_item + 2: [at_key],
        3 * per_item + 3: [at_style_key],
        3 * per_item + 4: [functools.partial(score_part, 0)],
        3 * per_item + 5: [functools.partial(score_part, 1)],
        3 * per_item + 6: [functools.partial(score_part, 2)],
        3 * per_item + 7: [functools.partial(score_part, 3)],
        4 * per_item + 2: [at_value],
        4 * per_item + 3: [at_style_value],
        4 * per_item + 5: [attend],
    }

    for index in range(total + 2):
        ring_step(index)
        if index == 0:
            for item in range(ITEMS):
                ref = slot(item, lon, 2)
                send(ref, ref, own_send.at[item], own_recv.at[item], sibling)
            for k, device in enumerate(peers):
                ref = tokens.at[tp]
                send(ref, ref, tp_send.at[0, k], tp_recv.at[0, k], device)
        for hook in hooks.get(index, ()):
            hook()

    await_sibling(4)
    wide = 512 if outw % 512 == 0 else outw

    def columns_of(owner, at):
        rows = pl.ds(pl.multiple_of(owner * outw + at * wide, 16), wide)
        return lax.dot_general(
            attended[...], weights[3, rows, :], NT, preferred_element_type=jnp.float32
        )

    for k, device in enumerate(peers):
        for at in range(outw // wide):
            cols = slice(at * wide, (at + 1) * wide)
            part[k, :, cols] = columns_of(lax.rem(tp + 1 + k, n_tp), at).astype(jnp.bfloat16)
            span = pl.ds(at * wide, wide)
            send(
                part.at[k, :, span],
                arrived.at[k, :, span],
                out_send.at[k, at],
                out_recv.at[k, at],
                device,
            )
    for at in range(outw // wide):
        cols = slice(at * wide, (at + 1) * wide)
        acc = columns_of(tp, at)
        for k, device in enumerate(peers):
            ref = arrived.at[k, :, pl.ds(at * wide, wide)]
            await_recv(ref, out_send.at[k, at], out_recv.at[k, at], device)
            acc = acc + arrived[k, :, cols].astype(jnp.float32)
        mixed_ref[:, cols] = acc.astype(jnp.bfloat16)
    for copy in started:
        copy.wait_send()


def local(n_lon, n_tp, image_tokens, style_tokens, qkv_weight, out_weight, query_gain, key_gain, attend_flags):
    count, feat = image_tokens.shape
    style_rows = style_tokens.shape[0]
    block, width = qkv_weight.shape[1:]
    outw = block * n_lon // n_tp
    key_count = 3 * count + style_rows * n_lon
    chips = n_lon // 2
    pieces = ITEMS * (chips - 1)
    peers = n_tp - 1
    tiles = outw // 512 if outw % 512 == 0 else 1
    bf16 = jnp.bfloat16
    vmem = pl.BlockSpec(memory_space=pltpu.VMEM)
    dma = pltpu.SemaphoreType.DMA
    return pl.pallas_call(
        functools.partial(kernel, n_lon, n_tp),
        out_shape=jax.ShapeDtypeStruct((count, outw), bf16),
        in_specs=[vmem] * 6 + [pl.BlockSpec(memory_space=pltpu.SMEM)],
        out_specs=vmem,
        scratch_shapes=[
            pltpu.VMEM((n_tp, count, feat), bf16),
            pltpu.VMEM((n_tp, 2, chips, style_rows, feat), bf16),
            pltpu.VMEM((4, block * n_lon, width), bf16),
            pltpu.VMEM((count, width), bf16),
            pltpu.VMEM((key_count, width), bf16),
            pltpu.VMEM((key_count, width), bf16),
            pltpu.VMEM((width // HEAD, count, key_count), bf16),
            pltpu.VMEM((count, width), bf16),
            pltpu.VMEM((peers, count, outw), bf16),
            pltpu.VMEM((peers, count, outw), bf16),
            dma((2, pieces)),
            dma((2, pieces)),
            dma((2, pieces)),
            dma((2, pieces)),
            dma((ITEMS,)),
            dma((ITEMS,)),
            dma((2, peers)),
            dma((2, peers)),
            dma((2, 2)),
            dma((2, 2)),
            dma((peers,)),
            dma((peers,)),
            dma((peers, tiles)),
            dma((peers, tiles)),
        ],
        compiler_params=pltpu.CompilerParams(
            collective_id=0, has_side_effects=True, vmem_limit_bytes=60 * 1024 * 1024
        ),
    )(
        image_tokens,
        style_tokens,
        qkv_weight,
        out_weight.T,
        query_gain.reshape(1, HEAD),
        key_gain.reshape(1, HEAD),
        attend_flags,
    )


def solution(mesh):
    in_specs = (
        P("lon", "tp"),
        P("lon", "tp"),
        P(None, "lon", "tp"),
        P("tp", "lon"),
        P(),
        P(),
        P("lon", None),
    )
    inner = functools.partial(local, mesh.shape["lon"], mesh.shape["tp"])
    return jax.shard_map(
        inner, mesh=mesh, in_specs=in_specs, out_specs=P("lon", "tp"), check_vma=False
    )
```

time: 293 us -> 186 us (0.63)
  waiting for transfers between devices: 219 us -> 0 us
  Pallas kernels: 0 us -> 184 us
  matrix products: 35.1 us -> 0 us
  between operations: 14 us -> 0.66 us
  local copies, waits for them, and re-layouts: 9.95 us -> 2.06 us
  blocking collectives: 6.69 us -> 0 us
  other arithmetic: 4.58 us -> 0 us
  starting transfers between devices: 3.89 us -> 0 us
    pallas_call x0 -> x1, Pallas kernels: none -> 184 us  [local(): pl.pallas_call(functools.partial(kernel, n_lon, n_tp), out_shape=jax.Shap...]
    all_gather x4 -> x0, waiting for transfers between devices: 176 us -> none  [the longest x1 95.8 us: local(): panel = lax.all_gather(qkv_weight, 'lon', axis=1, tiled=True)]
    dot_general x4 -> x0, matrix products: 27.6 us -> none  [the longest x1 9.77 us: local(): jnp.einsum('td,jdc->jtc', image_full, panel, preferred_element_type=jnp.f...]
    reduce_scatter x1 -> x0, waiting for transfers between devices: 24.8 us -> none  [local(): lax.psum_scatter(partial_sums.astype(jnp.bfloat16), 'tp', scatter_dimensi...]
    ppermute x2 -> x0, waiting for transfers between devices: 15.6 us -> none  [the longest x1 11.1 us: with_halo(): lax.ppermute(lax.slice_in_dim(block, 0, width, axis=dim), axis, backward)]
    sub x1 -> x0, matrix products: 7.48 us -> none  [local(): expo = jnp.exp(scores - peak)]
    all_gather x1 -> x0, blocking collectives: 6.69 us -> none  [local(): lax.all_gather(style_tokens, 'tp', axis=1, tiled=True)]
    ppermute x2 -> x0, starting transfers between devices: 3.73 us -> none  [the longest x1 3.73 us: with_halo(): lax.ppermute(lax.slice_in_dim(block, 0, width, axis=dim), axis, backward)]
  transfers between devices with their start and end apart: 7 -> 0, of which waited for: 7 -> 0; matrix products, arithmetic and copies ran while one was open for 14% -> 0% of each run, Pallas kernels for 0% -> 0%
where the time goes in v1:
time: 186 us
  Pallas kernels  184 us (99%)
  local copies, waits for them, and re-layouts  2.06 us (1%)
    pallas_call x1, Pallas kernels, local(): pl.pallas_call(functools.partial(kernel, n_lon, n_tp), out_shape=jax.Shap...  184 us

profile of v1, /device:TPU:0, one launch (start us, length us, event | category | flops | bytes accessed | tf_op | source)
XLA Modules:
  0.0 186.3 jit_solution(14227912045034832568)
XLA Ops:
  0.7 183.6 %shard_map.73 = bf16[256,1536]{1,0:T(8,128)(2,1)} custom-call(bf16[256,1536]{1,0:T(8,128)(2,1)} %image_ref.1, bf16[32,1536]{1,0:T(8,128)(2,1)} %style_ref.1, bf16[3,192,1024]{2,1,0:T(8,128)(2,1)} %qkv_ref.1, bf16[192,1024]{1,0:T(8,128)(2,1)} %bitcast.3, f32[1,128]{1,0:T(1,128)} %bitcast.4, f32[1,128]{1,0:T(1,128)} %bitcast.5, s32[1,1]{1,0:T(1,128)S(6)} %copy.9.flags_ref), custom_call_target="tpu_custom_call" | custom-call | tf_op jit(solution)/shard_map/pallas_call | solution.py:385
  184.2 2.1 %copy.10 = bf16[256,1536]{1,0:T(8,128)(2,1)} copy(bf16[256,1536]{1,0:T(8,128)(2,1)} %shard_map.73) | data formatting | bytes 1572864

commit v2 on v1

--- a/solution.py
+++ b/solution.py
@@ -10,6 +10,7 @@
 
 HEAD = 128
 ITEMS = 5
+WHERE = {1: 1, 2: 0, 3: 2, 4: 3}
 MESH = pl.DeviceIdType.MESH
 NT = (((1,), (1,)), ((), ()))
 
@@ -60,9 +61,9 @@
     width = qkv_ref.shape[2]
     heads = width // HEAD
     key_count = keys.shape[0]
-    outw = mixed_ref.shape[1]
     chips = n_lon // 2
     half_ring = chips // 2
+    share = chips // n_tp
     lon = lax.axis_index("lon")
     tp = lax.axis_index("tp")
     chip = lon // 2
@@ -94,7 +95,7 @@
         start, size = {0: (0, low), 1: (low, total - low), 2: (0, total)}[half]
         if item == 0:
             return styles.at[tp, owner % 2, owner // 2, pl.ds(start, size), :]
-        return weights.at[item - 1, pl.ds(pl.multiple_of(owner * block, 16) + start, size), :]
+        return weights.at[WHERE[item], pl.ds(pl.multiple_of(owner * block, 16) + start, size), :]
 
     barrier = pltpu.get_barrier_semaphore()
     partners = [right, left, sibling, after, before] + peers
@@ -167,22 +168,30 @@
                     device,
                 )
 
-    def await_sibling(item):
-        ref = slot(item, chip * 2 + 1 - core, 2)
-        await_recv(ref, own_send.at[item], own_recv.at[item], sibling)
+    def await_hop(item, hops):
+        if hops == 0:
+            ref = slot(item, chip * 2 + 1 - core, 2)
+            await_recv(ref, own_send.at[item], own_recv.at[item], sibling)
         for at in range(per_item):
             index = item * per_item + at
             for direction in range(2):
                 _, hop, half = piece(index, direction)
+                if hop + 1 != hops:
+                    continue
                 ref = slot(item, origin(hop + 1, direction, 1 - core), half)
                 await_recv(
                     ref, sib_send.at[direction, index], sib_recv.at[direction, index], sibling
                 )
 
+    def await_sibling(item):
+        for hops in range(half_ring + 1):
+            await_hop(item, hops)
+
     tile = 512 if width % 512 == 0 else width
-
-    def project(source, j, write):
-        @pl.loop(0, width // tile)
+    tiles = width // tile
+
+    def project(source, j, write, first=0, last=tiles):
+        @pl.loop(first, last)
         def _(at):
             start = pl.multiple_of(at * tile, tile)
             acc = None
@@ -243,10 +252,7 @@
             send(ref, ref, tp_send.at[1, k], tp_recv.at[1, k], device)
 
     def at_query():
-        await_sibling(1)
-        for k, device in enumerate(peers):
-            ref = tokens.at[lax.rem(tp + n_tp - 1 - k, n_tp)]
-            await_recv(ref, tp_send.at[0, k], tp_recv.at[0, k], device)
+        await_sibling(2)
         project(own_tokens, 0, write_normed(queries, 0, query_gain_ref))
 
     def at_style_peers():
@@ -256,16 +262,22 @@
             send(ref, ref, fwd_send.at[k], fwd_recv.at[k], sibling)
 
     def at_key():
-        await_sibling(2)
+        await_sibling(1)
+        for k, device in enumerate(peers):
+            ref = tokens.at[lax.rem(tp + n_tp - 1 - k, n_tp)]
+            await_recv(ref, tp_send.at[0, k], tp_recv.at[0, k], device)
         project(own_tokens, 1, write_normed(keys, count, key_gain_ref))
         send_halo(keys, 0)
 
-    def at_style_key():
-        await_sibling(0)
-        for k in range(n_tp - 1):
-            ref = styles.at[lax.rem(tp + n_tp - 1 - k, n_tp), 1 - core]
-            await_recv(ref, fwd_send.at[k], fwd_recv.at[k], sibling)
-        project(style_tokens_of, 1, write_normed(keys, 3 * count, key_gain_ref))
+    def at_style_key(at):
+        if at == 0:
+            await_sibling(0)
+            for k in range(n_tp - 1):
+                ref = styles.at[lax.rem(tp + n_tp - 1 - k, n_tp), 1 - core]
+                await_recv(ref, fwd_send.at[k], fwd_recv.at[k], sibling)
+        project(
+            style_tokens_of, 1, write_normed(keys, 3 * count, key_gain_ref), at, at + 1
+        )
 
     def score(first, last):
         bias = jnp.where(flags_ref[0, 0] > 0, 0.0, -1e30).astype(jnp.float32)
@@ -288,8 +300,8 @@
         project(own_tokens, 2, write_plain(values, count))
         send_halo(values, 1)
 
-    def at_style_value():
-        project(style_tokens_of, 2, write_plain(values, 3 * count))
+    def at_style_value(at):
+        project(style_tokens_of, 2, write_plain(values, 3 * count), at, at + 1)
 
     def attend():
         await_halo(values, 1)
@@ -301,28 +313,59 @@
                 probs[h], values[:, cols], preferred_element_type=jnp.float32
             ).astype(jnp.bfloat16)
 
-    pair = max(heads // 4, 1)
-
-    def score_part(quarter):
-        if quarter == 0:
+    def score_part(at):
+        if at == 0:
             await_halo(keys, 0)
-        if quarter * pair < heads:
-            score(quarter * pair, quarter * pair + pair)
-
-    hooks = {
-        per_item + 2: [at_style],
-        2 * per_item + 2: [at_query],
-        2 * per_item + 4: [at_style_peers],
-        3 * per_item + 2: [at_key],
-        3 * per_item + 3: [at_style_key],
-        3 * per_item + 4: [functools.partial(score_part, 0)],
-        3 * per_item + 5: [functools.partial(score_part, 1)],
-        3 * per_item + 6: [functools.partial(score_part, 2)],
-        3 * per_item + 7: [functools.partial(score_part, 3)],
-        4 * per_item + 2: [at_value],
-        4 * per_item + 3: [at_style_value],
-        4 * per_item + 5: [attend],
-    }
+        first, last = heads * at // (per_item - 1), heads * (at + 1) // (per_item - 1)
+        if first < last:
+            score(first, last)
+
+    def out_block(place_of):
+        origin_chip = lon_at(place_of, 0) // 2
+        rows = pl.ds(pl.multiple_of(origin_chip * (2 * block), 16), 2 * block)
+        part[origin_chip] = lax.dot_general(
+            attended[...], weights[3, rows, :], NT, preferred_element_type=jnp.float32
+        ).astype(jnp.bfloat16)
+        owner = origin_chip // share
+        at = lax.rem(origin_chip, share)
+
+        @pl.when(owner != tp)
+        def _():
+            k = lax.rem(owner - tp + n_tp, n_tp) - 1
+            pltpu.make_async_remote_copy(
+                src_ref=part.at[origin_chip],
+                dst_ref=arrived.at[k, at],
+                send_sem=out_send.at[k, at],
+                recv_sem=out_recv.at[k, at],
+                device_id={"tp": owner},
+                device_id_type=MESH,
+            ).start()
+
+    def out_hop(hops):
+        await_hop(4, hops)
+        out_block(place - hops)
+        if 0 < hops < half_ring:
+            out_block(place + hops)
+
+    hooks = {}
+
+    def plan(index, hook, *args):
+        hooks.setdefault(index, []).append(functools.partial(hook, *args))
+
+    plan(per_item + 1, at_style)
+    plan(2 * per_item + 1, at_style_peers)
+    plan(2 * per_item + 2, at_key)
+    for at in range(tiles):
+        plan(2 * per_item + 4 + at, at_style_key, at)
+        plan(4 * per_item + 3 + at, at_style_value, at)
+    plan(3 * per_item + 2, at_query)
+    for at in range(per_item - 1):
+        plan(3 * per_item + 3 + at, score_part, at)
+    plan(4 * per_item + 2, at_value)
+    plan(4 * per_item + 3 + tiles, attend)
+    for hops in range(half_ring + 1):
+        when = max(4 * per_item + 3 + tiles, 4 * per_item + 2 * hops + 2)
+        plan(min(when, total + 1), out_hop, hops)
 
     for index in range(total + 2):
         ring_step(index)
@@ -336,35 +379,24 @@
         for hook in hooks.get(index, ()):
             hook()
 
-    await_sibling(4)
-    wide = 512 if outw % 512 == 0 else outw
-
-    def columns_of(owner, at):
-        rows = pl.ds(pl.multiple_of(owner * outw + at * wide, 16), wide)
-        return lax.dot_general(
-            attended[...], weights[3, rows, :], NT, preferred_element_type=jnp.float32
-        )
-
+    for at in range(share):
+        acc = part[tp * share + at].astype(jnp.float32)
+        for k, device in enumerate(peers):
+            ref = arrived.at[k, at]
+            await_recv(ref, out_send.at[k, at], out_recv.at[k, at], device)
+            acc = acc + arrived[k, at].astype(jnp.float32)
+        mixed_ref[at] = acc.astype(jnp.bfloat16)
     for k, device in enumerate(peers):
-        for at in range(outw // wide):
-            cols = slice(at * wide, (at + 1) * wide)
-            part[k, :, cols] = columns_of(lax.rem(tp + 1 + k, n_tp), at).astype(jnp.bfloat16)
-            span = pl.ds(at * wide, wide)
-            send(
-                part.at[k, :, span],
-                arrived.at[k, :, span],
-                out_send.at[k, at],
-                out_recv.at[k, at],
-                device,
-            )
-    for at in range(outw // wide):
-        cols = slice(at * wide, (at + 1) * wide)
-        acc = columns_of(tp, at)
-        for k, device in enumerate(peers):
-            ref = arrived.at[k, :, pl.ds(at * wide, wide)]
-            await_recv(ref, out_send.at[k, at], out_recv.at[k, at], device)
-            acc = acc + arrived[k, :, cols].astype(jnp.float32)
-        mixed_ref[:, cols] = acc.astype(jnp.bfloat16)
+        owner = lax.rem(tp + 1 + k, n_tp)
+        for at in range(share):
+            pltpu.make_async_remote_copy(
+                src_ref=part.at[owner * share + at],
+                dst_ref=arrived.at[k, at],
+                send_sem=out_send.at[k, at],
+                recv_sem=out_recv.at[k, at],
+                device_id=device,
+                device_id_type=MESH,
+            ).wait_send()
     for copy in started:
         copy.wait_send()
 
@@ -378,13 +410,13 @@
     chips = n_lon // 2
     pieces = ITEMS * (chips - 1)
     peers = n_tp - 1
-    tiles = outw // 512 if outw % 512 == 0 else 1
+    share = chips // n_tp
     bf16 = jnp.bfloat16
     vmem = pl.BlockSpec(memory_space=pltpu.VMEM)
     dma = pltpu.SemaphoreType.DMA
-    return pl.pallas_call(
+    mixed = pl.pallas_call(
         functools.partial(kernel, n_lon, n_tp),
-        out_shape=jax.ShapeDtypeStruct((count, outw), bf16),
+        out_shape=jax.ShapeDtypeStruct((share, count, 2 * block), bf16),
         in_specs=[vmem] * 6 + [pl.BlockSpec(memory_space=pltpu.SMEM)],
         out_specs=vmem,
         scratch_shapes=[
@@ -396,8 +428,8 @@
             pltpu.VMEM((key_count, width), bf16),
             pltpu.VMEM((width // HEAD, count, key_count), bf16),
             pltpu.VMEM((count, width), bf16),
-            pltpu.VMEM((peers, count, outw), bf16),
-            pltpu.VMEM((peers, count, outw), bf16),
+            pltpu.VMEM((chips, count, 2 * block), bf16),
+            pltpu.VMEM((peers, share, count, 2 * block), bf16),
             dma((2, pieces)),
             dma((2, pieces)),
             dma((2, pieces)),
@@ -410,8 +442,8 @@
             dma((2, 2)),
             dma((peers,)),
             dma((peers,)),
-            dma((peers, tiles)),
-            dma((peers, tiles)),
+            dma((peers, share)),
+            dma((peers, share)),
         ],
         compiler_params=pltpu.CompilerParams(
             collective_id=0, has_side_effects=True, vmem_limit_bytes=60 * 1024 * 1024
@@ -425,6 +457,7 @@
         key_gain.reshape(1, HEAD),
         attend_flags,
     )
+    return mixed.transpose(1, 0, 2).reshape(count, outw)
 
 
 def solution(mesh):

time: 186 us -> 179 us (0.962)
  Pallas kernels: 184 us -> 175 us
    pallas_call x1, Pallas kernels: 184 us -> 175 us  [local(): pl.pallas_call(functools.partial(kernel, n_lon, n_tp), out_shape=jax.Shap...]
    unnamed x1 -> x0, local copies, waits for them, and re-layouts: 2.06 us -> none
where the time goes in v2:
time: 179 us; the launch traced here: 178 us
  Pallas kernels  175 us (98%)
  local copies, waits for them, and re-layouts  2.56 us (1%)
    pallas_call x1, Pallas kernels, local(): pl.pallas_call(functools.partial(kernel, n_lon, n_tp), out_shape=jax.Shap...  175 us

profile of v2, /device:TPU:0, one launch (start us, length us, event | category | flops | bytes accessed | tf_op | source)
XLA Modules:
  0.0 178.3 jit_solution(7360355236258197397)
XLA Ops:
  0.7 175.1 %shard_map.73 = bf16[4,256,384]{2,1,0:T(8,128)(2,1)} custom-call(bf16[256,1536]{1,0:T(8,128)(2,1)} %image_ref.1, bf16[32,1536]{1,0:T(8,128)(2,1)} %style_ref.1, bf16[3,192,1024]{2,1,0:T(8,128)(2,1)} %qkv_ref.1, bf16[192,1024]{1,0:T(8,128)(2,1)} %bitcast.7, f32[1,128]{1,0:T(1,128)} %bitcast.8, f32[1,128]{1,0:T(1,128)} %bitcast.9, s32[1,1]{1,0:T(1,128)S(6)} %copy.10.flags_ref), custom_call_target="tpu_custom_call" | custom-call | tf_op jit(solution)/shard_map/pallas_call | solution.py:417
  175.7 1.4 copy.8
  177.1 1.2 copy.9
